TPU v7x, 32 devices: a whole 2x2x4 slice. The times are simulated.
32 devices in a mesh: depth: 4 (over y, x), au: 4 (over z), vert: 2 (over core).
Axes of the slice: x: 2, y: 2, z: 4, core: 2. Of those that a mesh axis runs over, the one named last changes fastest.
Arguments:
- density: float32 [64, 512, 256], P('depth', 'au', 'vert'), may hold values from 0.3 to 3
- image_cotangent: float32 [2, 512, 256], P(None, 'au', 'vert'), may hold values from -6 to 6
- shear_rows: int32 [64], P('depth'), may hold values from -16 to 16, as said below
- shear_cols: int32 [64], P('depth'), may hold values from -16 to 16, as said below
- velocity_code: int32 [2, 64, 512, 256], P(None, 'depth', 'au', 'vert'), may hold values from 0 to 26
- limiter: int32 [2, 64, 512, 256], P(None, 'depth', 'au', 'vert'), may hold values 0 or 1
Outputs:
- density_cotangent: float32 [64, 512, 256], P('depth', 'au', 'vert')
Inputs may be any that keep to these rules, and one draw needn't show every extreme that they name: `shear_rows`: both values -16 and 16 occur in every draw. `shear_cols`: both values -16 and 16 occur in every draw.
All inputs are finite; a program needn't handle non-finite values. No bound on the sum of `limiter` on one device may be relied on, other than what follows from the above.
Results may differ from a plain program's by a relative error of at most 0.0003.
Values sent between devices are 32-bit elements; how exact they have to be, the bound alone decides.
A program may use at most 64 MiB of HBM per device.

v0:
```python
import functools

import jax
import jax.numpy as jnp
from jax import lax
from jax.experimental import pallas as pl
from jax.experimental.pallas import tpu as pltpu
from jax.sharding import PartitionSpec as P

SHEAR = 16
OPTICAL = 1.7
FRACTIONS = (0.3, 0.6, 0.45)
MESH = pl.DeviceIdType.MESH
HALO = 8
ROWS = 32


def remote(src, dst, send, recv, device):
    return pltpu.make_async_remote_copy(
        src_ref=src, dst_ref=dst, send_sem=send, recv_sem=recv, device_id=device, device_id_type=MESH
    )


def blend(taps, low, mid, frac):
    first = jnp.where(low, taps[0], jnp.where(mid, taps[1], taps[2]))
    second = jnp.where(low, taps[1], jnp.where(mid, taps[2], taps[3]))
    return (1.0 - frac) * first + frac * second


def masks_v(code):
    return code < 9, code < 18


def rest_u(code):
    return code - jnp.where(code < 9, 0, jnp.where(code < 18, 9, 18))


def masks_u(code):
    rest = rest_u(code)
    return rest < 3, rest < 6


def masks_z(code):
    rest = rest_u(code)
    rest = rest - jnp.where(rest < 3, 0, jnp.where(rest < 6, 3, 6))
    return rest < 1, rest < 2


def kernel(
    sizes, rows_ref, cols_ref, dens, image, codes, limits, out,
    brick, code, lim, img, xs, es, ts, grad0, grad1, cots, kepts, tu, tz, res,
    tl, gath, pr, back,
    ds_s, ds_r, dh_s, dh_r, lc, cs_s, cs_r, is_s, is_r, ga_s, ga_r, bk_s, bk_r,
    gh_s, gh_r, us, ur, zs, zr, os_s, os_r,
):
    D, A, V = sizes
    nz, nu, nv = dens.shape
    steps = codes.shape[0]
    nub, nvf = nu // V, nv * V
    d, a, c = lax.axis_index("depth"), lax.axis_index("au"), lax.axis_index("vert")
    p = a * V + c
    has_prev, has_next = p > 0, p < A * V - 1
    prev = {"au": lax.div(p - 1 + V, V) - 1, "vert": lax.rem(p - 1 + V, V)}
    nxt = {"au": lax.div(p + 1, V), "vert": lax.rem(p + 1, V)}
    delta = OPTICAL / (nz * D)

    barrier = pltpu.get_barrier_semaphore()

    def greet(device):
        pl.semaphore_signal(barrier, inc=1, device_id=device, device_id_type=MESH)

    for k in range(1, V):
        greet({"vert": lax.rem(c + k, V)})
    for k in range(1, D):
        greet({"depth": lax.rem(d + k, D)})

    @pl.when(a > 0)
    def _():
        for w in range(V):
            greet({"au": a - 1, "vert": w})

    @pl.when(a < A - 1)
    def _():
        for w in range(V):
            greet({"au": a + 1, "vert": w})

    beside = jnp.minimum(a, 1) + jnp.minimum(A - 1 - a, 1)
    pl.semaphore_wait(barrier, V - 1 + D - 1 + V * beside)

    def cut(w):
        return max(0, w * nub - SHEAR), min(nu, w * nub + nub + SHEAR)

    def lanes(w):
        return pl.ds(w * nv, nv)

    def to_brick(w, frm):
        lo, hi = cut(w)
        at = lo - w * nub + SHEAR
        return dens.at[:, lo:hi, :], brick.at[:, at:at + hi - lo, lanes(frm)]

    def block(source, target, w, frm):
        return source.at[..., w * nub:(w + 1) * nub, :], target.at[..., lanes(frm)]

    def each_core(action):
        for mine in range(V):
            pl.when(c == mine)(functools.partial(action, mine))

    def inputs(mine):
        local = [pltpu.make_async_copy(*to_brick(mine, mine), lc.at[0])]
        local.append(pltpu.make_async_copy(*block(image, img, mine, mine), lc.at[1]))
        for s in range(steps):
            local.append(pltpu.make_async_copy(*block(codes.at[s], code.at[s], mine, mine), lc.at[2 + 2 * s]))
            local.append(pltpu.make_async_copy(*block(limits.at[s], lim.at[s], mine, mine), lc.at[3 + 2 * s]))
        return local

    def start_inputs(mine):
        @pl.when(a > 0)
        def _():
            remote(dens.at[:, :SHEAR, :], brick.at[:, SHEAR + nub:, lanes(mine)], dh_s.at[0], dh_r.at[0, mine],
                   {"au": a - 1, "vert": V - 1}).start()

        @pl.when(a < A - 1)
        def _():
            remote(dens.at[:, nu - SHEAR:, :], brick.at[:, :SHEAR, lanes(mine)], dh_s.at[1], dh_r.at[1, mine],
                   {"au": a + 1, "vert": 0}).start()

        others = [w for w in range(V) if w != mine]
        for w in others:
            remote(*to_brick(w, mine), ds_s.at[w], ds_r.at[mine], {"vert": w}).start()
        local = inputs(mine)
        for one in local:
            one.start()
        for w in others:
            remote(*block(image, img, w, mine), is_s.at[w], is_r.at[mine], {"vert": w}).start()
        for s in range(steps - 1, -1, -1):
            for w in others:
                remote(*block(limits.at[s], lim.at[s], w, mine), cs_s.at[s, 1, w], cs_r.at[s, 1, mine], {"vert": w}).start()
                remote(*block(codes.at[s], code.at[s], w, mine), cs_s.at[s, 0, w], cs_r.at[s, 0, mine], {"vert": w}).start()

    each_core(start_inputs)

    @pl.when(jnp.logical_not(has_prev))
    def _():
        brick[:, :SHEAR, :] = jnp.zeros((nz, SHEAR, nvf), jnp.float32)
        grad0[:, :SHEAR, :] = jnp.zeros((nz, SHEAR, nvf), jnp.float32)
        for e in range(2 * steps):
            tu[e, :, :HALO, :] = jnp.zeros((nz, HALO, nvf), jnp.float32)

    @pl.when(jnp.logical_not(has_next))
    def _():
        brick[:, SHEAR + nub:, :] = jnp.zeros((nz, SHEAR, nvf), jnp.float32)
        grad0[:, SHEAR + nub:, :] = jnp.zeros((nz, SHEAR, nvf), jnp.float32)
        for e in range(2 * steps):
            tu[e, :, HALO + nub:, :] = jnp.zeros((nz, HALO, nvf), jnp.float32)

    @pl.when(d == 0)
    def _():
        for e in range(2 * steps):
            tz[e, :2] = jnp.zeros((2, nub, nvf), jnp.float32)

    @pl.when(d == D - 1)
    def _():
        for e in range(2 * steps):
            tz[e, nz + 2:] = jnp.zeros((2, nub, nvf), jnp.float32)

    def wait_brick(mine):
        inputs(mine)[0].wait()
        for w in range(V):
            if w != mine:
                lo, hi = cut(mine)
                at = lo - mine * nub + SHEAR
                here = brick.at[:, at:at + hi - lo, lanes(w)]
                remote(here, here, ds_s.at[w], ds_r.at[w], {"vert": w}).wait_recv()
        if mine == V - 1:
            @pl.when(a < A - 1)
            def _():
                for w in range(V):
                    here = brick.at[:, SHEAR + nub:, lanes(w)]
                    remote(here, here, dh_s.at[0], dh_r.at[0, w], {"au": a + 1, "vert": w}).wait_recv()
        if mine == 0:
            @pl.when(a > 0)
            def _():
                for w in range(V):
                    here = brick.at[:, :SHEAR, lanes(w)]
                    remote(here, here, dh_s.at[1], dh_r.at[1, w], {"au": a - 1, "vert": w}).wait_recv()

    each_core(wait_brick)

    column = lax.broadcasted_iota(jnp.int32, (ROWS, nvf), 1)

    def moved(values, by):
        rolled = pltpu.roll(values, lax.rem(nvf - by, nvf), 1)
        at = column + by
        return jnp.where((at >= 0) & (at < nvf), rolled, 0.0)

    chunks = [(r, pl.ds(r, ROWS)) for r in range(0, nub, ROWS)]

    def shifted(ref, z, r, by):
        span = ROWS + 2 * SHEAR
        rows = ref[z, pl.ds(r, span), :]
        return pltpu.roll(rows, lax.rem(span - SHEAR - by, span), 0)[:ROWS]

    for view in range(2):
        for r, here in chunks:
            def ahead(z, carry, view=view, r=r, here=here):
                trans, light = carry
                if view == 0:
                    x = shifted(brick, z, r, rows_ref[z])
                else:
                    x = moved(brick[z, pl.ds(SHEAR + r, ROWS), :], cols_ref[z])
                e = jnp.exp(-delta * x)
                xs[view, z, here, :] = x
                es[view, z, here, :] = e
                ts[view, z, here, :] = trans
                return trans * e, light + trans * (1.0 - e) * x

            ones = jnp.ones((ROWS, nvf), jnp.float32)
            trans, light = lax.fori_loop(0, nz, ahead, (ones, jnp.zeros_like(ones)))
            tl[0, pl.ds(view * nub + r, ROWS), :] = trans
            tl[1, pl.ds(view * nub + r, ROWS), :] = light

    part = 2 * nub // D

    def at_part(k):
        return pl.ds(pl.multiple_of(k * part, part), part)

    def gather(k):
        peer = lax.rem(d + k, D)
        return remote(tl.at[:, at_part(peer), :], gath.at[d], ga_s.at[k], ga_r.at[k], {"depth": peer})

    for k in range(1, D):
        gather(k).start()
    gath[d] = tl[:, at_part(d), :]
    for k in range(1, D):
        here = gath.at[lax.rem(d - k + D, D)]
        remote(here, here, ga_s.at[k], ga_r.at[k], {"depth": lax.rem(d - k + D, D)}).wait_recv()
    run = jnp.ones((part, nvf), jnp.float32)
    for k in range(D):
        pr[k, 0] = run
        run = run * gath[k, 0]
    run = jnp.zeros((part, nvf), jnp.float32)
    for k in range(D - 1, -1, -1):
        pr[k, 1] = run
        run = gath[k, 1] + gath[k, 0] * run

    def give(k):
        peer = lax.rem(d + k, D)
        return remote(pr.at[peer], back.at[:, at_part(d), :], bk_s.at[k], bk_r.at[k], {"depth": peer})

    for k in range(1, D):
        give(k).start()
    back[:, at_part(d), :] = pr[d]

    def wait_image(mine):
        inputs(mine)[1].wait()
        for w in range(V):
            if w != mine:
                here = img.at[..., lanes(w)]
                remote(here, here, is_s.at[w], is_r.at[w], {"vert": w}).wait_recv()

    each_core(wait_image)
    for k in range(1, D):
        here = back.at[:, at_part(lax.rem(d - k + D, D)), :]
        remote(here, here, bk_s.at[k], bk_r.at[k], {"depth": lax.rem(d - k + D, D)}).wait_recv()

    def grad_up():
        return remote(grad0.at[:, SHEAR:2 * SHEAR, :], grad0.at[:, SHEAR + nub:, :], gh_s.at[0], gh_r.at[0], prev)

    def grad_down():
        return remote(grad0.at[:, nub:nub + SHEAR, :], grad0.at[:, :SHEAR, :], gh_s.at[1], gh_r.at[1], nxt)

    for view in range(2):
        for r, here in chunks:
            mine = pl.ds(view * nub + r, ROWS)
            before = back[0, mine, :]
            weight = img[view, here, :]
            later = before * tl[0, mine, :] * back[1, mine, :]

            def behind(k, later, view=view, r=r, here=here, before=before, weight=weight):
                z = nz - 1 - k
                x, e = xs[view, z, here, :], es[view, z, here, :]
                trans = before * ts[view, z, here, :]
                opacity = 1.0 - e
                grad = weight * (trans * (e * x + opacity * (1.0 / delta)) - later)
                if view == 0:
                    grad0[z, pl.ds(SHEAR + r, ROWS), :] = grad
                else:
                    grad1[z, here, :] = grad
                return later + trans * opacity * x

            lax.fori_loop(0, nz, behind, later)
        if view == 0:
            @pl.when(has_prev)
            def _():
                grad_up().start()

            @pl.when(has_next)
            def _():
                grad_down().start()

    def wait_codes(mine):
        for one in inputs(mine)[2:]:
            one.wait()
        for s in range(steps):
            for w in range(V):
                if w != mine:
                    for kind, target in ((0, code), (1, lim)):
                        here = target.at[s, ..., lanes(w)]
                        remote(here, here, cs_s.at[s, kind, w], cs_r.at[s, kind, w], {"vert": w}).wait_recv()

    each_core(wait_codes)

    @pl.when(has_next)
    def _():
        grad_up().wait_recv()

    @pl.when(has_prev)
    def _():
        grad_down().wait_recv()

    middle = nz // 2
    groups = ((0, 2), (nz - 2, nz), (2, middle), (middle, nz - 2))
    edges_first, edges_last = (0, 1, 2, 3), (2, 3, 0, 1)

    def u_up(e, g):
        lo, hi = groups[g]
        return remote(tu.at[e, lo:hi, HALO:2 * HALO, :], tu.at[e, lo:hi, HALO + nub:, :],
                      us.at[e, g, 0], ur.at[e, g, 0], prev)

    def u_down(e, g):
        lo, hi = groups[g]
        return remote(tu.at[e, lo:hi, nub:nub + HALO, :], tu.at[e, lo:hi, :HALO, :],
                      us.at[e, g, 1], ur.at[e, g, 1], nxt)

    def u_start(e, g):
        @pl.when(has_prev)
        def _():
            u_up(e, g).start()

        @pl.when(has_next)
        def _():
            u_down(e, g).start()

    def u_wait(e, g):
        @pl.when(has_next)
        def _():
            u_up(e, g).wait_recv()

        @pl.when(has_prev)
        def _():
            u_down(e, g).wait_recv()

    def z_up(e):
        after = 1 + e % 2
        return remote(tz.at[e, 2:2 + after], tz.at[e, nz + 2:nz + 2 + after], zs.at[e, 0], zr.at[e, 0], {"depth": d - 1})

    def z_down(e):
        before = 2 - e % 2
        return remote(tz.at[e, nz + 2 - before:nz + 2], tz.at[e, 2 - before:2], zs.at[e, 1], zr.at[e, 1], {"depth": d + 1})

    def z_start(e):
        @pl.when(d > 0)
        def _():
            z_up(e).start()

        @pl.when(d < D - 1)
        def _():
            z_down(e).start()

    def z_wait(e):
        @pl.when(d < D - 1)
        def _():
            z_up(e).wait_recv()

        @pl.when(d > 0)
        def _():
            z_down(e).wait_recv()

    def over(g, body):
        lo, hi = groups[g]

        def one(z, carry):
            for r, here in chunks:
                body(z, r, here)
            return carry

        lax.fori_loop(lo, hi, one, 0)

    def v_sweep(values, cells, sign):
        taps = [values if n == 0 else moved(values, sign * n) for n in (-1, 0, 1, 2)]
        return blend(taps, *masks_v(cells), FRACTIONS[2])

    def open_step(n, z, r, here, cot):
        s = steps - 1 - n
        cots[n, z, here, :] = cot
        kept = jnp.where(lim[s, z, here, :] == 0, 0.5 * cot, 0.0)
        kepts[n, z, here, :] = kept
        tu[2 * n, z, pl.ds(HALO + r, ROWS), :] = v_sweep(kept, code[s, z, here, :], -1)

    def first(z, r, here):
        cot = shifted(grad0, z, r, -rows_ref[z]) + moved(grad1[z, here, :], -cols_ref[z])
        open_step(0, z, r, here, cot)

    for g in edges_first:
        over(g, first)
        u_start(0, g)

    def out_copy(mine, w, g):
        lo, hi = groups[g]
        return res.at[lo:hi, :, lanes(w)], out.at[lo:hi, mine * nub:(mine + 1) * nub, :]

    def out_start(g, mine):
        pltpu.make_async_copy(*out_copy(mine, mine, g), os_s.at[g, mine]).start()
        for w in range(V):
            if w != mine:
                remote(*out_copy(mine, w, g), os_s.at[g, w], os_r.at[g, mine], {"vert": w}).start()

    for n in range(steps):
        s = steps - 1 - n
        for half in range(2):
            e, sign = 2 * n + half, 2 * half - 1

            def u_body(z, r, here, e=e, sign=sign, s=s):
                taps = [tu[e, z, pl.ds(HALO + r + sign * k, ROWS), :] for k in (-1, 0, 1, 2)]
                tz[e, z + 2, here, :] = blend(taps, *masks_u(code[s, z, here, :]), FRACTIONS[1])

            for i, g in enumerate(edges_first):
                u_wait(e, g)
                over(g, u_body)
                if i == 1:
                    z_start(e)

            def z_body(z, r, here, e=e, sign=sign, s=s, n=n, half=half):
                cells = code[s, z, here, :]
                taps = [tz[e, z + 2 + sign * k, here, :] for k in (-1, 0, 1, 2)]
                swept = blend(taps, *masks_z(cells), FRACTIONS[0])
                if half == 0:
                    hat = cots[n, z, here, :] - swept
                    tu[e + 1, z, pl.ds(HALO + r, ROWS), :] = v_sweep(hat, cells, 1)
                elif n < steps - 1:
                    open_step(n + 1, z, r, here, kepts[n, z, here, :] + swept)
                else:
                    res[z, here, :] = kepts[n, z, here, :] + swept

            for i, g in enumerate(edges_last):
                if i == 2:
                    z_wait(e)
                over(g, z_body)
                if e + 1 < 2 * steps:
                    u_start(e + 1, g)
                else:
                    each_core(functools.partial(out_start, g))

    def drain(mine):
        for g in range(len(groups)):
            pltpu.make_async_copy(*out_copy(mine, mine, g), os_s.at[g, mine]).wait()
            lo, hi = groups[g]
            for w in range(V):
                if w != mine:
                    remote(*out_copy(mine, w, g), os_s.at[g, w], os_r.at[g, mine], {"vert": w}).wait_send()
                    here = out.at[lo:hi, w * nub:(w + 1) * nub, :]
                    remote(here, here, os_s.at[g, w], os_r.at[g, w], {"vert": w}).wait_recv()
        for w in range(V):
            if w != mine:
                remote(*to_brick(w, mine), ds_s.at[w], ds_r.at[mine], {"vert": w}).wait_send()
                remote(*block(image, img, w, mine), is_s.at[w], is_r.at[mine], {"vert": w}).wait_send()
                for s in range(steps):
                    remote(*block(codes.at[s], code.at[s], w, mine), cs_s.at[s, 0, w], cs_r.at[s, 0, mine], {"vert": w}).wait_send()
                    remote(*block(limits.at[s], lim.at[s], w, mine), cs_s.at[s, 1, w], cs_r.at[s, 1, mine], {"vert": w}).wait_send()

        @pl.when(a > 0)
        def _():
            remote(dens.at[:, :SHEAR, :], brick.at[:, SHEAR + nub:, lanes(mine)], dh_s.at[0], dh_r.at[0, mine],
                   {"au": a - 1, "vert": V - 1}).wait_send()

        @pl.when(a < A - 1)
        def _():
            remote(dens.at[:, nu - SHEAR:, :], brick.at[:, :SHEAR, lanes(mine)], dh_s.at[1], dh_r.at[1, mine],
                   {"au": a + 1, "vert": 0}).wait_send()

    each_core(drain)
    for k in range(1, D):
        gather(k).wait_send()
        give(k).wait_send()

    @pl.when(has_prev)
    def _():
        grad_up().wait_send()
        for e in range(2 * steps):
            for g in range(len(groups)):
                u_up(e, g).wait_send()

    @pl.when(has_next)
    def _():
        grad_down().wait_send()
        for e in range(2 * steps):
            for g in range(len(groups)):
                u_down(e, g).wait_send()

    @pl.when(d > 0)
    def _():
        for e in range(2 * steps):
            z_up(e).wait_send()

    @pl.when(d < D - 1)
    def _():
        for e in range(2 * steps):
            z_down(e).wait_send()


def per_device(sizes, density, image_cotangent, shear_rows, shear_cols, velocity_code, limiter):
    D, A, V = sizes
    nz, nu, nv = density.shape
    steps = velocity_code.shape[0]
    nub, nvf = nu // V, nv * V
    f32, i32 = jnp.float32, jnp.int32
    vmem, dma = pltpu.VMEM, pltpu.SemaphoreType.DMA
    part = 2 * nub // D
    scratch = [
        vmem((nz, nub + 2 * SHEAR, nvf), f32),
        vmem((steps, nz, nub, nvf), i32),
        vmem((steps, nz, nub, nvf), i32),
        vmem((2, nub, nvf), f32),
        vmem((2, nz, nub, nvf), f32),
        vmem((2, nz, nub, nvf), f32),
        vmem((2, nz, nub, nvf), f32),
        vmem((nz, nub + 2 * SHEAR, nvf), f32),
        vmem((nz, nub, nvf), f32),
        vmem((steps, nz, nub, nvf), f32),
        vmem((steps, nz, nub, nvf), f32),
        vmem((2 * steps, nz, nub + 2 * HALO, nvf), f32),
        vmem((2 * steps, nz + 4, nub, nvf), f32),
        vmem((nz, nub, nvf), f32),
        vmem((2, 2 * nub, nvf), f32),
        vmem((D, 2, part, nvf), f32),
        vmem((D, 2, part, nvf), f32),
        vmem((2, 2 * nub, nvf), f32),
        dma((V,)), dma((V,)), dma((2,)), dma((2, V)), dma((2 + 2 * steps,)),
        dma((steps, 2, V)), dma((steps, 2, V)), dma((V,)), dma((V,)),
        dma((D,)), dma((D,)), dma((D,)), dma((D,)),
        dma((2,)), dma((2,)),
        dma((2 * steps, 4, 2)), dma((2 * steps, 4, 2)),
        dma((2 * steps, 2)), dma((2 * steps, 2)),
        dma((4, V)), dma((4, V)),
    ]
    smem = pl.BlockSpec(memory_space=pltpu.SMEM)
    far = pl.BlockSpec(memory_space=pl.ANY)
    return pl.pallas_call(
        functools.partial(kernel, sizes),
        out_shape=jax.ShapeDtypeStruct(density.shape, f32),
        in_specs=[smem, smem, far, far, far, far],
        out_specs=far,
        scratch_shapes=scratch,
        compiler_params=pltpu.CompilerParams(
            collective_id=0, has_side_effects=True, vmem_limit_bytes=56 * 1024 * 1024
        ),
    )(shear_rows, shear_cols, density, image_cotangent, velocity_code, limiter)


def solution(mesh):
    placed = (
        P("depth", "au", "vert"),
        P(None, "au", "vert"),
        P("depth"),
        P("depth"),
        P(None, "depth", "au", "vert"),
        P(None, "depth", "au", "vert"),
    )
    sizes = tuple(mesh.shape[name] for name in ("depth", "au", "vert"))
    return jax.shard_map(
        functools.partial(per_device, sizes), mesh=mesh, in_specs=placed,
        out_specs=P("depth", "au", "vert"), check_vma=False,
    )
```

profile of v0, /device:TPU:19, one launch (start us, length us, event | category | flops | bytes accessed | tf_op | source)
XLA Modules:
  0.0 67.4 jit_solution(4718591101271907922)
XLA Ops:
  0.0 65.1 %shard_map.64 = f32[16,128,128]{2,1,0:T(8,128)} custom-call(s32[16]{0:T(128)} %rows_ref.1, s32[16]{0:T(128)} %cols_ref.1, f32[16,128,128]{2,1,0:T(8,128)} %dens.1, f32[2,128,128]{2,1,0:T(8,128)} %image.1, s32[2,16,128,128]{3,2,1,0:T(8,128)} %codes.1, s32[2,16,128,128]{3,2,1,0:T(8,128)} %limits.1), custom_call_target="tpu_custom_call" | custom-call | tf_op jit(solution)/shard_map/pallas_call | solution.py:548
  65.1 2.3 %copy.8 = f32[16,128,128]{2,1,0:T(8,128)} copy(f32[16,128,128]{2,1,0:T(8,128)} %shard_map.64) | data formatting | bytes 2097152
where the time goes:
time: 67.6 us; the launch traced here: 67.4 us
  Pallas kernels  65.1 us (96%)
  local copies, waits for them, and re-layouts  2.3 us (3%)
    pallas_call x1, Pallas kernels, per_device(): pl.pallas_call(functools.partial(kernel, sizes), out_shape=jax.ShapeDtype...  65.1 us
    unnamed x1, local copies, waits for them, and re-layouts  2.3 us

commit v1 on v0

--- a/solution.py
+++ b/solution.py
@@ -27,29 +27,18 @@
     return (1.0 - frac) * first + frac * second
 
 
-def masks_v(code):
-    return code < 9, code < 18
-
-
-def rest_u(code):
-    return code - jnp.where(code < 9, 0, jnp.where(code < 18, 9, 18))
-
-
-def masks_u(code):
-    rest = rest_u(code)
+def masks_u(rest):
     return rest < 3, rest < 6
 
 
-def masks_z(code):
-    rest = rest_u(code)
-    rest = rest - jnp.where(rest < 3, 0, jnp.where(rest < 6, 3, 6))
+def masks_z(rest):
     return rest < 1, rest < 2
 
 
 def kernel(
     sizes, rows_ref, cols_ref, dens, image, codes, limits, out,
     brick, code, lim, img, xs, es, ts, grad0, grad1, cots, kepts, tu, tz, res,
-    tl, gath, pr, back,
+    tl, gath, pr, back, codeu, codez,
     ds_s, ds_r, dh_s, dh_r, lc, cs_s, cs_r, is_s, is_r, ga_s, ga_r, bk_s, bk_r,
     gh_s, gh_r, us, ur, zs, zr, os_s, os_r,
 ):
@@ -116,7 +105,7 @@
     def start_inputs(mine):
         @pl.when(a > 0)
         def _():
-            remote(dens.at[:, :SHEAR, :], brick.at[:, SHEAR + nub:, lanes(mine)], dh_s.at[0], dh_r.at[0, mine],
+            remote(dens.at[:, :SHEAR, :], brick.at[:, SHEAR + nub:2 * SHEAR + nub, lanes(mine)], dh_s.at[0], dh_r.at[0, mine],
                    {"au": a - 1, "vert": V - 1}).start()
 
         @pl.when(a < A - 1)
@@ -139,6 +128,9 @@
 
     each_core(start_inputs)
 
+    brick[:, 2 * SHEAR + nub:, :] = jnp.zeros((nz, 8, nvf), jnp.float32)
+    grad0[:, 2 * SHEAR + nub:, :] = jnp.zeros((nz, 8, nvf), jnp.float32)
+
     @pl.when(jnp.logical_not(has_prev))
     def _():
         brick[:, :SHEAR, :] = jnp.zeros((nz, SHEAR, nvf), jnp.float32)
@@ -148,8 +140,8 @@
 
     @pl.when(jnp.logical_not(has_next))
     def _():
-        brick[:, SHEAR + nub:, :] = jnp.zeros((nz, SHEAR, nvf), jnp.float32)
-        grad0[:, SHEAR + nub:, :] = jnp.zeros((nz, SHEAR, nvf), jnp.float32)
+        brick[:, SHEAR + nub:2 * SHEAR + nub, :] = jnp.zeros((nz, SHEAR, nvf), jnp.float32)
+        grad0[:, SHEAR + nub:2 * SHEAR + nub, :] = jnp.zeros((nz, SHEAR, nvf), jnp.float32)
         for e in range(2 * steps):
             tu[e, :, HALO + nub:, :] = jnp.zeros((nz, HALO, nvf), jnp.float32)
 
@@ -175,7 +167,7 @@
             @pl.when(a < A - 1)
             def _():
                 for w in range(V):
-                    here = brick.at[:, SHEAR + nub:, lanes(w)]
+                    here = brick.at[:, SHEAR + nub:2 * SHEAR + nub, lanes(w)]
                     remote(here, here, dh_s.at[0], dh_r.at[0, w], {"au": a + 1, "vert": w}).wait_recv()
         if mine == 0:
             @pl.when(a > 0)
@@ -186,12 +178,32 @@
 
     each_core(wait_brick)
 
-    column = lax.broadcasted_iota(jnp.int32, (ROWS, nvf), 1)
+    lane = lax.broadcasted_iota(jnp.int32, (ROWS, nv), 1)
+    row = lax.broadcasted_iota(jnp.int32, (8, nvf), 0)
+    nothing = jnp.zeros((ROWS, nv), jnp.float32)
+
+    def tiles(values):
+        return [nothing] + [values[:, w * nv:(w + 1) * nv] for w in range(V)] + [nothing]
+
+    def joined(parts):
+        return jnp.concatenate(parts, axis=1)
+
+    def tap(parts, by):
+        turned = [pltpu.roll(one, (-by) % nv, 1) for one in parts[1:-1]]
+        turned = [nothing] + turned + [nothing]
+        if by > 0:
+            inside = lane < nv - by
+            return [jnp.where(inside, turned[w], turned[w + 1]) for w in range(1, V + 1)]
+        inside = lane >= -by
+        return [jnp.where(inside, turned[w], turned[w - 1]) for w in range(1, V + 1)]
 
     def moved(values, by):
-        rolled = pltpu.roll(values, lax.rem(nvf - by, nvf), 1)
-        at = column + by
-        return jnp.where((at >= 0) & (at < nvf), rolled, 0.0)
+        turned = [pltpu.roll(one, lax.rem(nv - by, nv), 1) for one in tiles(values)[1:-1]]
+        turned = [nothing] + turned + [nothing]
+        at = lane + by
+        return joined([
+            jnp.where(at < 0, turned[w - 1], jnp.where(at < nv, turned[w], turned[w + 1])) for w in range(1, V + 1)
+        ])
 
     chunks = [(r, pl.ds(r, ROWS)) for r in range(0, nub, ROWS)]
 
@@ -199,6 +211,28 @@
         span = ROWS + 2 * SHEAR
         rows = ref[z, pl.ds(r, span), :]
         return pltpu.roll(rows, lax.rem(span - SHEAR - by, span), 0)[:ROWS]
+
+    part = V * nub // D
+
+    def at_part(k):
+        return pl.ds(pl.multiple_of(k * part, part), part)
+
+    def gather(view, k):
+        peer = lax.rem(d + k, D)
+        return remote(tl.at[view, :, at_part(peer), :], gath.at[view, d], ga_s.at[view, k], ga_r.at[view, k],
+                      {"depth": peer})
+
+    def give(view, k):
+        peer = lax.rem(d + k, D)
+        return remote(pr.at[view, peer], back.at[view, :, at_part(d), :], bk_s.at[view, k], bk_r.at[view, k],
+                      {"depth": peer})
+
+    def put(view, kind, r, values):
+        for w in range(V):
+            tl[view, kind, pl.ds(w * nub + r, ROWS), :] = values[:, w * nv:(w + 1) * nv]
+
+    def get(ref, view, kind, r):
+        return joined([ref[view, kind, pl.ds(w * nub + r, ROWS), :] for w in range(V)])
 
     for view in range(2):
         for r, here in chunks:
@@ -212,91 +246,36 @@
                 xs[view, z, here, :] = x
                 es[view, z, here, :] = e
                 ts[view, z, here, :] = trans
-                return trans * e, light + trans * (1.0 - e) * x
+                left = trans * e
+                return left, light + (trans - left) * x
+
+            def ahead_pair(k, carry, ahead=ahead):
+                return ahead(2 * k + 1, ahead(2 * k, carry))
 
             ones = jnp.ones((ROWS, nvf), jnp.float32)
-            trans, light = lax.fori_loop(0, nz, ahead, (ones, jnp.zeros_like(ones)))
-            tl[0, pl.ds(view * nub + r, ROWS), :] = trans
-            tl[1, pl.ds(view * nub + r, ROWS), :] = light
-
-    part = 2 * nub // D
-
-    def at_part(k):
-        return pl.ds(pl.multiple_of(k * part, part), part)
-
-    def gather(k):
-        peer = lax.rem(d + k, D)
-        return remote(tl.at[:, at_part(peer), :], gath.at[d], ga_s.at[k], ga_r.at[k], {"depth": peer})
-
-    for k in range(1, D):
-        gather(k).start()
-    gath[d] = tl[:, at_part(d), :]
-    for k in range(1, D):
-        here = gath.at[lax.rem(d - k + D, D)]
-        remote(here, here, ga_s.at[k], ga_r.at[k], {"depth": lax.rem(d - k + D, D)}).wait_recv()
-    run = jnp.ones((part, nvf), jnp.float32)
-    for k in range(D):
-        pr[k, 0] = run
-        run = run * gath[k, 0]
-    run = jnp.zeros((part, nvf), jnp.float32)
-    for k in range(D - 1, -1, -1):
-        pr[k, 1] = run
-        run = gath[k, 1] + gath[k, 0] * run
-
-    def give(k):
-        peer = lax.rem(d + k, D)
-        return remote(pr.at[peer], back.at[:, at_part(d), :], bk_s.at[k], bk_r.at[k], {"depth": peer})
-
-    for k in range(1, D):
-        give(k).start()
-    back[:, at_part(d), :] = pr[d]
-
-    def wait_image(mine):
-        inputs(mine)[1].wait()
-        for w in range(V):
-            if w != mine:
-                here = img.at[..., lanes(w)]
-                remote(here, here, is_s.at[w], is_r.at[w], {"vert": w}).wait_recv()
-
-    each_core(wait_image)
-    for k in range(1, D):
-        here = back.at[:, at_part(lax.rem(d - k + D, D)), :]
-        remote(here, here, bk_s.at[k], bk_r.at[k], {"depth": lax.rem(d - k + D, D)}).wait_recv()
-
-    def grad_up():
-        return remote(grad0.at[:, SHEAR:2 * SHEAR, :], grad0.at[:, SHEAR + nub:, :], gh_s.at[0], gh_r.at[0], prev)
-
-    def grad_down():
-        return remote(grad0.at[:, nub:nub + SHEAR, :], grad0.at[:, :SHEAR, :], gh_s.at[1], gh_r.at[1], nxt)
+            trans, light = lax.fori_loop(0, nz // 2, ahead_pair, (ones, jnp.zeros_like(ones)))
+            put(view, 0, r, trans)
+            put(view, 1, r, light)
+        for k in range(1, D):
+            gather(view, k).start()
+        gath[view, d] = tl[view, :, at_part(d), :]
 
     for view in range(2):
-        for r, here in chunks:
-            mine = pl.ds(view * nub + r, ROWS)
-            before = back[0, mine, :]
-            weight = img[view, here, :]
-            later = before * tl[0, mine, :] * back[1, mine, :]
-
-            def behind(k, later, view=view, r=r, here=here, before=before, weight=weight):
-                z = nz - 1 - k
-                x, e = xs[view, z, here, :], es[view, z, here, :]
-                trans = before * ts[view, z, here, :]
-                opacity = 1.0 - e
-                grad = weight * (trans * (e * x + opacity * (1.0 / delta)) - later)
-                if view == 0:
-                    grad0[z, pl.ds(SHEAR + r, ROWS), :] = grad
-                else:
-                    grad1[z, here, :] = grad
-                return later + trans * opacity * x
-
-            lax.fori_loop(0, nz, behind, later)
-        if view == 0:
-            @pl.when(has_prev)
-            def _():
-                grad_up().start()
-
-            @pl.when(has_next)
-            def _():
-                grad_down().start()
+        for k in range(1, D):
+            peer = lax.rem(d - k + D, D)
+            here = gath.at[view, peer]
+            remote(here, here, ga_s.at[view, k], ga_r.at[view, k], {"depth": peer}).wait_recv()
+        run = jnp.ones((part, nv), jnp.float32)
+        for k in range(D):
+            pr[view, k, 0] = run
+            run = run * gath[view, k, 0]
+        run = jnp.zeros((part, nv), jnp.float32)
+        for k in range(D - 1, -1, -1):
+            pr[view, k, 1] = run
+            run = gath[view, k, 1] + gath[view, k, 0] * run
+        for k in range(1, D):
+            give(view, k).start()
+        back[view, :, at_part(d), :] = pr[view, d]
 
     def wait_codes(mine):
         for one in inputs(mine)[2:]:
@@ -308,7 +287,71 @@
                         here = target.at[s, ..., lanes(w)]
                         remote(here, here, cs_s.at[s, kind, w], cs_r.at[s, kind, w], {"vert": w}).wait_recv()
 
+    def decode(s):
+        def one(z, carry):
+            for r, here in chunks:
+                cells = code[s, z, here, :]
+                rest = cells - jnp.where(cells < 9, 0, jnp.where(cells < 18, 9, 18))
+                codeu[s, z, here, :] = rest
+                codez[s, z, here, :] = rest - jnp.where(rest < 3, 0, jnp.where(rest < 6, 3, 6))
+            return carry
+
+        lax.fori_loop(0, nz, one, 0)
+
     each_core(wait_codes)
+    decode(steps - 1)
+
+    def wait_image(mine):
+        inputs(mine)[1].wait()
+        for w in range(V):
+            if w != mine:
+                here = img.at[..., lanes(w)]
+                remote(here, here, is_s.at[w], is_r.at[w], {"vert": w}).wait_recv()
+
+    each_core(wait_image)
+    def grad_up():
+        return remote(grad0.at[:, SHEAR:2 * SHEAR, :], grad0.at[:, SHEAR + nub:2 * SHEAR + nub, :], gh_s.at[0], gh_r.at[0], prev)
+
+    def grad_down():
+        return remote(grad0.at[:, nub:nub + SHEAR, :], grad0.at[:, :SHEAR, :], gh_s.at[1], gh_r.at[1], nxt)
+
+    for view in range(2):
+        for k in range(1, D):
+            peer = lax.rem(d - k + D, D)
+            here = back.at[view, :, at_part(peer), :]
+            remote(here, here, bk_s.at[view, k], bk_r.at[view, k], {"depth": peer}).wait_recv()
+        for r, here in chunks:
+            before = get(back, view, 0, r)
+            weight = img[view, here, :]
+            later = before * get(tl, view, 0, r) * get(back, view, 1, r)
+
+            def behind(z, later, view=view, r=r, here=here, before=before, weight=weight):
+                x, e = xs[view, z, here, :], es[view, z, here, :]
+                trans = before * ts[view, z, here, :]
+                left = trans * e
+                lost = trans - left
+                grad = weight * (left * x + lost * (1.0 / delta) - later)
+                if view == 0:
+                    grad0[z, pl.ds(SHEAR + r, ROWS), :] = grad
+                else:
+                    grad1[z, here, :] = grad
+                return later + lost * x
+
+            def behind_pair(k, later, behind=behind):
+                return behind(nz - 2 - 2 * k, behind(nz - 1 - 2 * k, later))
+
+            lax.fori_loop(0, nz // 2, behind_pair, later)
+            if view == 0 and r == 0:
+                @pl.when(has_prev)
+                def _():
+                    grad_up().start()
+        if view == 0:
+            @pl.when(has_next)
+            def _():
+                grad_down().start()
+
+    for s in range(steps - 1):
+        decode(s)
 
     @pl.when(has_next)
     def _():
@@ -379,16 +422,22 @@
     def over(g, body):
         lo, hi = groups[g]
 
-        def one(z, carry):
-            for r, here in chunks:
-                body(z, r, here)
+        def two(k, carry):
+            for z in (lo + 2 * k, lo + 2 * k + 1):
+                for r, here in chunks:
+                    body(z, r, here)
             return carry
 
-        lax.fori_loop(lo, hi, one, 0)
+        lax.fori_loop(0, (hi - lo) // 2, two, 0)
 
     def v_sweep(values, cells, sign):
-        taps = [values if n == 0 else moved(values, sign * n) for n in (-1, 0, 1, 2)]
-        return blend(taps, *masks_v(cells), FRACTIONS[2])
+        parts = tiles(values)
+        taps = [parts[1:-1] if n == 0 else tap(parts, sign * n) for n in (-1, 0, 1, 2)]
+        low, mid = cells < 9, cells < 18
+        return joined([
+            blend([one[w] for one in taps], low[:, w * nv:(w + 1) * nv], mid[:, w * nv:(w + 1) * nv], FRACTIONS[2])
+            for w in range(V)
+        ])
 
     def open_step(n, z, r, here, cot):
         s = steps - 1 - n
@@ -422,18 +471,19 @@
 
             def u_body(z, r, here, e=e, sign=sign, s=s):
                 taps = [tu[e, z, pl.ds(HALO + r + sign * k, ROWS), :] for k in (-1, 0, 1, 2)]
-                tz[e, z + 2, here, :] = blend(taps, *masks_u(code[s, z, here, :]), FRACTIONS[1])
-
-            for i, g in enumerate(edges_first):
+                tz[e, z + 2, here, :] = blend(taps, *masks_u(codeu[s, z, here, :]), FRACTIONS[1])
+
+            order = edges_first if e == 0 else (2, 0, 1, 3)
+            for g in order:
                 u_wait(e, g)
                 over(g, u_body)
-                if i == 1:
+                if g == 1:
                     z_start(e)
 
             def z_body(z, r, here, e=e, sign=sign, s=s, n=n, half=half):
                 cells = code[s, z, here, :]
                 taps = [tz[e, z + 2 + sign * k, here, :] for k in (-1, 0, 1, 2)]
-                swept = blend(taps, *masks_z(cells), FRACTIONS[0])
+                swept = blend(taps, *masks_z(codez[s, z, here, :]), FRACTIONS[0])
                 if half == 0:
                     hat = cots[n, z, here, :] - swept
                     tu[e + 1, z, pl.ds(HALO + r, ROWS), :] = v_sweep(hat, cells, 1)
@@ -470,7 +520,7 @@
 
         @pl.when(a > 0)
         def _():
-            remote(dens.at[:, :SHEAR, :], brick.at[:, SHEAR + nub:, lanes(mine)], dh_s.at[0], dh_r.at[0, mine],
+            remote(dens.at[:, :SHEAR, :], brick.at[:, SHEAR + nub:2 * SHEAR + nub, lanes(mine)], dh_s.at[0], dh_r.at[0, mine],
                    {"au": a - 1, "vert": V - 1}).wait_send()
 
         @pl.when(a < A - 1)
@@ -479,9 +529,10 @@
                    {"au": a + 1, "vert": 0}).wait_send()
 
     each_core(drain)
-    for k in range(1, D):
-        gather(k).wait_send()
-        give(k).wait_send()
+    for view in range(2):
+        for k in range(1, D):
+            gather(view, k).wait_send()
+            give(view, k).wait_send()
 
     @pl.when(has_prev)
     def _():
@@ -515,29 +566,31 @@
     nub, nvf = nu // V, nv * V
     f32, i32 = jnp.float32, jnp.int32
     vmem, dma = pltpu.VMEM, pltpu.SemaphoreType.DMA
-    part = 2 * nub // D
+    part = V * nub // D
     scratch = [
-        vmem((nz, nub + 2 * SHEAR, nvf), f32),
+        vmem((nz, nub + 2 * SHEAR + 8, nvf), f32),
         vmem((steps, nz, nub, nvf), i32),
         vmem((steps, nz, nub, nvf), i32),
         vmem((2, nub, nvf), f32),
         vmem((2, nz, nub, nvf), f32),
         vmem((2, nz, nub, nvf), f32),
         vmem((2, nz, nub, nvf), f32),
-        vmem((nz, nub + 2 * SHEAR, nvf), f32),
+        vmem((nz, nub + 2 * SHEAR + 8, nvf), f32),
         vmem((nz, nub, nvf), f32),
         vmem((steps, nz, nub, nvf), f32),
         vmem((steps, nz, nub, nvf), f32),
         vmem((2 * steps, nz, nub + 2 * HALO, nvf), f32),
         vmem((2 * steps, nz + 4, nub, nvf), f32),
         vmem((nz, nub, nvf), f32),
-        vmem((2, 2 * nub, nvf), f32),
-        vmem((D, 2, part, nvf), f32),
-        vmem((D, 2, part, nvf), f32),
-        vmem((2, 2 * nub, nvf), f32),
+        vmem((2, 2, V * nub, nv), f32),
+        vmem((2, D, 2, part, nv), f32),
+        vmem((2, D, 2, part, nv), f32),
+        vmem((2, 2, V * nub, nv), f32),
+        vmem((steps, nz, nub, nvf), i32),
+        vmem((steps, nz, nub, nvf), i32),
         dma((V,)), dma((V,)), dma((2,)), dma((2, V)), dma((2 + 2 * steps,)),
         dma((steps, 2, V)), dma((steps, 2, V)), dma((V,)), dma((V,)),
-        dma((D,)), dma((D,)), dma((D,)), dma((D,)),
+        dma((2, D)), dma((2, D)), dma((2, D)), dma((2, D)),
         dma((2,)), dma((2,)),
         dma((2 * steps, 4, 2)), dma((2 * steps, 4, 2)),
         dma((2 * steps, 2)), dma((2 * steps, 2)),

time: 67.6 us -> 60.3 us (0.89)
  Pallas kernels: 65.1 us -> 57.8 us
    pallas_call x1, Pallas kernels: 65.1 us -> 57.8 us  [per_device(): pl.pallas_call(functools.partial(kernel, sizes), out_shape=jax.ShapeDtype...]
where the time goes in v1:
time: 60.3 us; the launch traced here: 60.1 us
  Pallas kernels  57.8 us (96%)
  local copies, waits for them, and re-layouts  2.3 us (4%)
    pallas_call x1, Pallas kernels, per_device(): pl.pallas_call(functools.partial(kernel, sizes), out_shape=jax.ShapeDtype...  57.8 us
    unnamed x1, local copies, waits for them, and re-layouts  2.3 us

profile of v1, /device:TPU:19, one launch (start us, length us, event | category | flops | bytes accessed | tf_op | source)
XLA Modules:
  0.0 60.1 jit_solution(2588325764090345664)
XLA Ops:
  0.0 57.8 %shard_map.64 = f32[16,128,128]{2,1,0:T(8,128)} custom-call(s32[16]{0:T(128)} %rows_ref.1, s32[16]{0:T(128)} %cols_ref.1, f32[16,128,128]{2,1,0:T(8,128)} %dens.1, f32[2,128,128]{2,1,0:T(8,128)} %image.1, s32[2,16,128,128]{3,2,1,0:T(8,128)} %codes.1, s32[2,16,128,128]{3,2,1,0:T(8,128)} %limits.1), custom_call_target="tpu_custom_call" | custom-call | tf_op jit(solution)/shard_map/pallas_call | solution.py:601
  57.8 2.3 %copy.8 = f32[16,128,128]{2,1,0:T(8,128)} copy(f32[16,128,128]{2,1,0:T(8,128)} %shard_map.64) | data formatting | bytes 2097152
